TPU v7x, 32 devices: a whole 2x2x4 slice. The times are simulated.
32 devices in a mesh: dp: 4 (over y, x), fsdp: 8 (over z, core).
Axes of the slice: x: 2, y: 2, z: 4, core: 2. Of those that a mesh axis runs over, the one named last changes fastest.
Arguments:
- tokens: bfloat16 [40960, 640], P(('dp', 'fsdp')), may hold values from -6 to 6
- lengths: int32 [32], P(('dp', 'fsdp')), may hold values from 500 to 1250, as said below
- query_weight: bfloat16 [768, 768], P('fsdp'), may hold values from -0.25 to 0.25
- key_weight: bfloat16 [768, 768], P('fsdp'), may hold values from -0.25 to 0.25
- value_weight: bfloat16 [768, 768], P('fsdp'), may hold values from -0.25 to 0.25
- out_weight: bfloat16 [768, 768], P('fsdp'), may hold values from -1 to 1
- up_weight: bfloat16 [768, 3072], P('fsdp'), may hold values from -0.25 to 0.25
- down_weight: bfloat16 [3072, 768], P('fsdp'), may hold values from -0.125 to 0.125
- query_bias: bfloat16 [768], P('fsdp'), may hold values from -3 to 3
- value_bias: bfloat16 [768], P('fsdp'), may hold values from -3 to 3
- out_bias: bfloat16 [768], P('fsdp'), may hold values from -3 to 3
- up_bias: bfloat16 [3072], P('fsdp'), may hold values from -3 to 3
- down_bias: bfloat16 [768], P('fsdp'), may hold values from -3 to 3
- first_gain: bfloat16 [768], P('fsdp'), may hold values from 0.099609375 to 1.8984375
- first_shift: bfloat16 [768], P('fsdp'), may hold values from -2 to 2
- second_gain: bfloat16 [768], P('fsdp'), may hold values from 0.099609375 to 1.8984375
- second_shift: bfloat16 [768], P('fsdp'), may hold values from -2 to 2
- cotangent: bfloat16 [40960, 640], P(('dp', 'fsdp')), may hold values from -6 to 6
Outputs:
- output: bfloat16 [40960, 640], P(('dp', 'fsdp'))
- token_grad: bfloat16 [40960, 640], P(('dp', 'fsdp'))
- grad_query_weight: float32 [768, 768], P('fsdp')
- grad_key_weight: float32 [768, 768], P('fsdp')
- grad_value_weight: float32 [768, 768], P('fsdp')
- grad_out_weight: float32 [768, 768], P('fsdp')
- grad_up_weight: float32 [768, 3072], P('fsdp')
- grad_down_weight: float32 [3072, 768], P('fsdp')
- grad_query_bias: float32 [768], P('fsdp')
- grad_value_bias: float32 [768], P('fsdp')
- grad_out_bias: float32 [768], P('fsdp')
- grad_up_bias: float32 [3072], P('fsdp')
- grad_down_bias: float32 [768], P('fsdp')
- grad_first_gain: float32 [768], P('fsdp')
- grad_first_shift: float32 [768], P('fsdp')
- grad_second_gain: float32 [768], P('fsdp')
- grad_second_shift: float32 [768], P('fsdp')
Inputs may be any that keep to these rules, and one draw needn't show every extreme that they name: Utterance lengths in frames; the utterances of one dp index form one length bucket, longer on higher indices; the longest is exactly 1250.
All inputs are finite; a program needn't handle non-finite values.
Results may differ from a plain program's by a relative error of at most 0.018.
Values may be sent and summed in bfloat16 or wider, within the bound.
No kernel may reach another device: no remote copies, remote signals or barrier semaphores. Data moves between devices by JAX's collectives and lax.ppermute only.
A program may use at most 256 MiB of HBM per device.

v0:
```python
import jax
import jax.numpy as jnp
from jax import lax
from jax.sharding import PartitionSpec as P

SUPER_WIDTH = 768
SUPER_HIDDEN = 3072
HEAD_DIM = 64
HIDDEN_SIZE = 2240
WIDTH = 640


EPSILON = 1e-05
MASKED = -1e30


def norm_rows(hidden, gain_row, shift_row):
    center = hidden - jnp.mean(hidden, -1, keepdims=True)
    spread = jnp.mean(center * center, -1, keepdims=True)
    return center * lax.rsqrt(spread + EPSILON) * gain_row + shift_row


def exact_gelu(values):
    return jax.nn.gelu(values, approximate=False)


def matmul(left_side, right_side, pattern):
    return jnp.einsum(pattern, left_side, right_side, preferred_element_type=jnp.float32)


def leading(fetched):
    return (
        fetched[0][:WIDTH],
        fetched[1][:WIDTH],
        fetched[2][:WIDTH],
        fetched[3][:WIDTH],
        fetched[4][:WIDTH],
        fetched[5][:HIDDEN_SIZE],
        fetched[6][:WIDTH].astype(jnp.float32),
        fetched[7][:WIDTH].astype(jnp.float32),
        fetched[8][:WIDTH].astype(jnp.float32),
        fetched[9][:HIDDEN_SIZE].astype(jnp.float32),
        fetched[10][:WIDTH].astype(jnp.float32),
        fetched[11][:WIDTH].astype(jnp.float32),
        fetched[12][:WIDTH].astype(jnp.float32),
        fetched[13][:WIDTH].astype(jnp.float32),
        fetched[14][:WIDTH].astype(jnp.float32),
    )


def head_scores(query_block, key_heads, keep_row):
    scores = matmul(query_block, key_heads, "qhd,khd->hqk") * HEAD_DIM ** (-0.5)
    return jnp.where(keep_row[None, None, :], scores, MASKED)


def attend_forward(query_rows, key_rows, value_rows, keep_row):
    length = query_rows.shape[0]
    head_count = query_rows.shape[1] // HEAD_DIM
    half_rows = length // 2
    key_heads = key_rows.reshape(length, head_count, HEAD_DIM)
    value_heads = value_rows.reshape(length, head_count, HEAD_DIM)
    query_blocks = query_rows.reshape(2, half_rows, head_count, HEAD_DIM)

    def one_block(query_block):
        scores = head_scores(query_block, key_heads, keep_row)
        highest = jnp.max(scores, -1, keepdims=True)
        log_total = highest + jnp.log(jnp.sum(jnp.exp(scores - highest), -1, keepdims=True))
        prob_low = jnp.exp(scores - log_total).astype(jnp.bfloat16)
        context = matmul(prob_low, value_heads, "hqk,khd->qhd")
        return (context.reshape(half_rows, head_count * HEAD_DIM), log_total)

    context, log_total = lax.map(one_block, query_blocks)
    return (context.reshape(length, head_count * HEAD_DIM).astype(jnp.bfloat16), log_total)


def attend_backward(query_rows, key_rows, value_rows, keep_row, log_total, grad_context):
    length = query_rows.shape[0]
    head_count = query_rows.shape[1] // HEAD_DIM
    half_rows = length // 2
    factor = HEAD_DIM ** (-0.5)
    key_heads = key_rows.reshape(length, head_count, HEAD_DIM)
    value_heads = value_rows.reshape(length, head_count, HEAD_DIM)
    query_blocks = query_rows.reshape(2, half_rows, head_count, HEAD_DIM)
    grad_blocks = grad_context.reshape(2, half_rows, head_count, HEAD_DIM)

    def one_block(running, pieces):
        grad_keys, grad_values = running
        query_block, grad_block, total_block = pieces
        scores = head_scores(query_block, key_heads, keep_row)
        prob_full = jnp.exp(scores - total_block)
        prob_low = prob_full.astype(jnp.bfloat16)
        grad_probs = matmul(grad_block, value_heads, "qhd,khd->hqk")
        weighted = jnp.sum(prob_full * grad_probs, -1, keepdims=True)
        grad_scores = (prob_full * (grad_probs - weighted)).astype(jnp.bfloat16)
        grad_query = matmul(grad_scores, key_heads, "hqk,khd->qhd") * factor
        grad_keys = grad_keys + matmul(grad_scores, query_block, "hqk,qhd->khd") * factor
        grad_values = grad_values + matmul(prob_low, grad_block, "hqk,qhd->khd")
        return ((grad_keys, grad_values), grad_query.reshape(half_rows, head_count * HEAD_DIM))

    empty_grad = jnp.zeros((length, head_count, HEAD_DIM), jnp.float32)
    (grad_keys, grad_values), grad_query = lax.scan(
        one_block, (empty_grad, empty_grad), (query_blocks, grad_blocks, log_total)
    )
    return (
        grad_query.reshape(length, -1),
        grad_keys.reshape(length, -1),
        grad_values.reshape(length, -1),
    )


def widen(matrix, row_count, column_count):
    return jnp.pad(matrix, ((0, row_count - matrix.shape[0]), (0, column_count - matrix.shape[1])))


def stretch(vector, count):
    return jnp.pad(vector, (0, count - vector.shape[0]))


def column_sums(matrix):
    return jnp.sum(matrix.astype(jnp.float32), 0)


def on_device(
    tokens,
    lengths,
    query_weight,
    key_weight,
    value_weight,
    out_weight,
    up_weight,
    down_weight,
    query_bias,
    value_bias,
    out_bias,
    up_bias,
    down_bias,
    first_gain,
    first_shift,
    second_gain,
    second_shift,
    cotangent,
):
    fetched = (
        lax.all_gather(query_weight[:, :WIDTH], "fsdp", axis=0, tiled=True),
        lax.all_gather(key_weight[:, :WIDTH], "fsdp", axis=0, tiled=True),
        lax.all_gather(value_weight[:, :WIDTH], "fsdp", axis=0, tiled=True),
        lax.all_gather(out_weight[:, :WIDTH], "fsdp", axis=0, tiled=True),
        lax.all_gather(up_weight[:, :HIDDEN_SIZE], "fsdp", axis=0, tiled=True),
        lax.all_gather(down_weight[:, :WIDTH], "fsdp", axis=0, tiled=True),
        lax.all_gather(query_bias, "fsdp", axis=0, tiled=True),
        lax.all_gather(value_bias, "fsdp", axis=0, tiled=True),
        lax.all_gather(out_bias, "fsdp", axis=0, tiled=True),
        lax.all_gather(up_bias, "fsdp", axis=0, tiled=True),
        lax.all_gather(down_bias, "fsdp", axis=0, tiled=True),
        lax.all_gather(first_gain, "fsdp", axis=0, tiled=True),
        lax.all_gather(first_shift, "fsdp", axis=0, tiled=True),
        lax.all_gather(second_gain, "fsdp", axis=0, tiled=True),
        lax.all_gather(second_shift, "fsdp", axis=0, tiled=True),
    )
    (
        query_sub,
        key_sub,
        value_sub,
        out_sub,
        up_sub,
        down_sub,
        query_add,
        value_add,
        out_add,
        up_add,
        down_add,
        gain_one,
        shift_one,
        gain_two,
        shift_two,
    ) = leading(fetched)
    row_count = tokens.shape[0]
    item_count = lengths.shape[0]
    slot_rows = row_count // item_count
    positions = lax.broadcasted_iota(jnp.int32, (item_count, slot_rows), 1)
    live_mask = positions < lengths[:, None]
    row_live = live_mask.reshape(row_count, 1).astype(jnp.float32)
    queries = (matmul(tokens, query_sub, "rw,wv->rv") + query_add).astype(jnp.bfloat16)
    key_rows = matmul(tokens, key_sub, "rw,wv->rv").astype(jnp.bfloat16)
    value_rows = (matmul(tokens, value_sub, "rw,wv->rv") + value_add).astype(jnp.bfloat16)
    member = 0
    context_part, total_part = attend_forward(queries, key_rows, value_rows, live_mask[member])
    total_parts = [total_part]
    branch = matmul(context_part, out_sub, "rw,wv->rv") + out_add
    first_sum = tokens.astype(jnp.float32) + branch
    normed_full, first_back = jax.vjp(norm_rows, first_sum, gain_one, shift_one)
    normed = normed_full.astype(jnp.bfloat16)
    hidden = matmul(normed, up_sub, "rw,wh->rh") + up_add
    active_full, gelu_back = jax.vjp(exact_gelu, hidden)
    active = active_full.astype(jnp.bfloat16)
    feed_out = matmul(active, down_sub, "rh,hw->rw") + down_add
    second_sum = normed.astype(jnp.float32) + feed_out
    result_full, second_back = jax.vjp(norm_rows, second_sum, gain_two, shift_two)
    output = (result_full * row_live).astype(jnp.bfloat16)
    refetched = (
        lax.all_gather(query_weight[:, :WIDTH], "fsdp", axis=0, tiled=True),
        lax.all_gather(key_weight[:, :WIDTH], "fsdp", axis=0, tiled=True),
        lax.all_gather(value_weight[:, :WIDTH], "fsdp", axis=0, tiled=True),
        lax.all_gather(out_weight[:, :WIDTH], "fsdp", axis=0, tiled=True),
        lax.all_gather(up_weight[:, :HIDDEN_SIZE], "fsdp", axis=0, tiled=True),
        lax.all_gather(down_weight[:, :WIDTH], "fsdp", axis=0, tiled=True),
        lax.all_gather(query_bias, "fsdp", axis=0, tiled=True),
        lax.all_gather(value_bias, "fsdp", axis=0, tiled=True),
        lax.all_gather(out_bias, "fsdp", axis=0, tiled=True),
        lax.all_gather(up_bias, "fsdp", axis=0, tiled=True),
        lax.all_gather(down_bias, "fsdp", axis=0, tiled=True),
        lax.all_gather(first_gain, "fsdp", axis=0, tiled=True),
        lax.all_gather(first_shift, "fsdp", axis=0, tiled=True),
        lax.all_gather(second_gain, "fsdp", axis=0, tiled=True),
        lax.all_gather(second_shift, "fsdp", axis=0, tiled=True),
    )
    (
        query_sub,
        key_sub,
        value_sub,
        out_sub,
        up_sub,
        down_sub,
        query_add,
        value_add,
        out_add,
        up_add,
        down_add,
        gain_one,
        shift_one,
        gain_two,
        shift_two,
    ) = leading(refetched)
    grad_result = cotangent.astype(jnp.float32) * row_live
    grad_second, grad_gain_two, grad_shift_two = second_back(grad_result)
    grad_feed = grad_second.astype(jnp.bfloat16)
    grad_active = matmul(grad_feed, down_sub, "rw,hw->rh")
    (grad_hidden_full,) = gelu_back(grad_active)
    grad_hidden = grad_hidden_full.astype(jnp.bfloat16)
    grad_normed = grad_second + matmul(grad_hidden, up_sub, "rh,wh->rw")
    grad_first, grad_gain_one, grad_shift_one = first_back(grad_normed)
    grad_branch = grad_first.astype(jnp.bfloat16)
    grad_context = matmul(grad_branch, out_sub, "rv,wv->rw").astype(jnp.bfloat16)
    member = 0
    grad_query_part, grad_key_part, grad_value_part = attend_backward(
        queries, key_rows, value_rows, live_mask[member], total_parts[member], grad_context
    )
    grad_queries = grad_query_part.astype(jnp.bfloat16)
    grad_keys = grad_key_part.astype(jnp.bfloat16)
    grad_values = grad_value_part.astype(jnp.bfloat16)
    token_grad = (
        grad_first
        + matmul(grad_queries, query_sub, "rv,wv->rw")
        + matmul(grad_keys, key_sub, "rv,wv->rw")
        + matmul(grad_values, value_sub, "rv,wv->rw")
    ).astype(jnp.bfloat16)
    query_term = matmul(tokens, grad_queries, "rw,rv->wv")
    key_term = matmul(tokens, grad_keys, "rw,rv->wv")
    value_term = matmul(tokens, grad_values, "rw,rv->wv")
    out_term = matmul(context_part, grad_branch, "rw,rv->wv")
    up_term = matmul(normed, grad_hidden, "rw,rh->wh")
    down_term = matmul(active, grad_feed, "rh,rw->hw")
    column_count = SUPER_WIDTH
    hidden_count = SUPER_HIDDEN
    summed = (
        lax.psum_scatter(
            widen(query_term, SUPER_WIDTH, column_count), "fsdp", scatter_dimension=0, tiled=True
        ),
        lax.psum_scatter(
            widen(key_term, SUPER_WIDTH, column_count), "fsdp", scatter_dimension=0, tiled=True
        ),
        lax.psum_scatter(
            widen(value_term, SUPER_WIDTH, column_count), "fsdp", scatter_dimension=0, tiled=True
        ),
        lax.psum_scatter(
            widen(out_term, SUPER_WIDTH, column_count), "fsdp", scatter_dimension=0, tiled=True
        ),
        lax.psum_scatter(
            widen(up_term, SUPER_WIDTH, hidden_count), "fsdp", scatter_dimension=0, tiled=True
        ),
        lax.psum_scatter(
            widen(down_term, SUPER_HIDDEN, column_count), "fsdp", scatter_dimension=0, tiled=True
        ),
        lax.psum_scatter(
            stretch(column_sums(grad_queries), SUPER_WIDTH), "fsdp", scatter_dimension=0, tiled=True
        ),
        lax.psum_scatter(
            stretch(column_sums(grad_values), SUPER_WIDTH), "fsdp", scatter_dimension=0, tiled=True
        ),
        lax.psum_scatter(
            stretch(column_sums(grad_branch), SUPER_WIDTH), "fsdp", scatter_dimension=0, tiled=True
        ),
        lax.psum_scatter(
            stretch(column_sums(grad_hidden), SUPER_HIDDEN), "fsdp", scatter_dimension=0, tiled=True
        ),
        lax.psum_scatter(
            stretch(column_sums(grad_feed), SUPER_WIDTH), "fsdp", scatter_dimension=0, tiled=True
        ),
        lax.psum_scatter(
            stretch(grad_gain_one, SUPER_WIDTH), "fsdp", scatter_dimension=0, tiled=True
        ),
        lax.psum_scatter(
            stretch(grad_shift_one, SUPER_WIDTH), "fsdp", scatter_dimension=0, tiled=True
        ),
        lax.psum_scatter(
            stretch(grad_gain_two, SUPER_WIDTH), "fsdp", scatter_dimension=0, tiled=True
        ),
        lax.psum_scatter(
            stretch(grad_shift_two, SUPER_WIDTH), "fsdp", scatter_dimension=0, tiled=True
        ),
    )
    totals = (
        lax.psum(summed[0].astype(jnp.bfloat16), "dp").astype(jnp.float32),
        lax.psum(summed[1].astype(jnp.bfloat16), "dp").astype(jnp.float32),
        lax.psum(summed[2].astype(jnp.bfloat16), "dp").astype(jnp.float32),
        lax.psum(summed[3].astype(jnp.bfloat16), "dp").astype(jnp.float32),
        lax.psum(summed[4].astype(jnp.bfloat16), "dp").astype(jnp.float32),
        lax.psum(summed[5].astype(jnp.bfloat16), "dp").astype(jnp.float32),
        lax.psum(summed[6].astype(jnp.bfloat16), "dp").astype(jnp.float32),
        lax.psum(summed[7].astype(jnp.bfloat16), "dp").astype(jnp.float32),
        lax.psum(summed[8].astype(jnp.bfloat16), "dp").astype(jnp.float32),
        lax.psum(summed[9].astype(jnp.bfloat16), "dp").astype(jnp.float32),
        lax.psum(summed[10].astype(jnp.bfloat16), "dp").astype(jnp.float32),
        lax.psum(summed[11].astype(jnp.bfloat16), "dp").astype(jnp.float32),
        lax.psum(summed[12].astype(jnp.bfloat16), "dp").astype(jnp.float32),
        lax.psum(summed[13].astype(jnp.bfloat16), "dp").astype(jnp.float32),
        lax.psum(summed[14].astype(jnp.bfloat16), "dp").astype(jnp.float32),
    )
    return (
        output,
        token_grad,
        widen(totals[0], totals[0].shape[0], SUPER_WIDTH),
        widen(totals[1], totals[1].shape[0], SUPER_WIDTH),
        widen(totals[2], totals[2].shape[0], SUPER_WIDTH),
        widen(totals[3], totals[3].shape[0], SUPER_WIDTH),
        widen(totals[4], totals[4].shape[0], SUPER_HIDDEN),
        widen(totals[5], totals[5].shape[0], SUPER_WIDTH),
        totals[6],
        totals[7],
        totals[8],
        totals[9],
        totals[10],
        totals[11],
        totals[12],
        totals[13],
        totals[14],
    )


def solution(mesh):
    placed = (
        P(("dp", "fsdp"), None),
        P(("dp", "fsdp")),
        P("fsdp", None),
        P("fsdp", None),
        P("fsdp", None),
        P("fsdp", None),
        P("fsdp", None),
        P("fsdp", None),
        P("fsdp"),
        P("fsdp"),
        P("fsdp"),
        P("fsdp"),
        P("fsdp"),
        P("fsdp"),
        P("fsdp"),
        P("fsdp"),
        P("fsdp"),
        P(("dp", "fsdp"), None),
    )
    return jax.shard_map(
        on_device,
        mesh=mesh,
        in_specs=placed,
        out_specs=(
            P(("dp", "fsdp"), None),
            P(("dp", "fsdp"), None),
            P("fsdp", None),
            P("fsdp", None),
            P("fsdp", None),
            P("fsdp", None),
            P("fsdp", None),
            P("fsdp", None),
            P("fsdp"),
            P("fsdp"),
            P("fsdp"),
            P("fsdp"),
            P("fsdp"),
            P("fsdp"),
            P("fsdp"),
            P("fsdp"),
            P("fsdp"),
        ),
        check_vma=False,
    )
```

profile of v0, /device:TPU:0, one launch (start us, length us, event | category | flops | bytes accessed | tf_op | source)
XLA Modules:
  0.0 1026.3 jit_solution(6105511377353195886)
XLA Ops:
  21.4 32.0 %all-reduce.33 = (bf16[768]{0:T(1024)(128)(2,1)S(1)}, bf16[768]{0:T(1024)(128)(2,1)S(1)}, bf16[768]{0:T(1024)(128)(2,1)S(1)}, bf16[768]{0:T(1024)(128)(2,1)}, bf...) all-reduce(bf16[768]{0:T(1024)(128)(2,1)S(1)} %dynamic-update-slice, ...), channel_id=1, replica_groups=mesh['dp'=4,'fsdp'=8] {'fsdp'}, use_global_device_ids=true, to_apply=%add.15 | all-reduce | flops 6144 | bytes 24576
  56.4 12.8 %all-gather = bf16[8,1,384]{2,1,0:T(2,128)(2,1)S(1)} all-gather(bf16[1,1,384]{2,1,0:T(2,128)(2,1)S(1)} %reshape.208), channel_id=1, replica_groups=mesh['dp'=4,'fsdp'=8] {'fsdp'}, dimensions={0}, use_global_device_ids=true | all-gather | bytes 6912 | tf_op jit(solution)/shard_map/all_gather | solution.py:153
  69.8 22.4 %all_gather.56 = bf16[768,640]{1,0:T(8,128)(2,1)} all-gather(bf16[96,640]{1,0:T(8,128)(2,1)S(1)} %slice-done.3), channel_id=1, replica_groups=mesh['dp'=4,'fsdp'=8] {'fsdp'}, dimensions={0}, use_global_device_ids=true | all-gather | bytes 1105920 | tf_op jit(solution)/shard_map/all_gather | solution.py:147
  92.2 22.4 %all_gather.54 = bf16[768,640]{1,0:T(8,128)(2,1)} all-gather(bf16[96,640]{1,0:T(8,128)(2,1)S(1)} %slice-done.2), channel_id=1, replica_groups=mesh['dp'=4,'fsdp'=8] {'fsdp'}, dimensions={0}, use_global_device_ids=true | all-gather | bytes 1105920 | tf_op jit(solution)/shard_map/all_gather | solution.py:146
  114.6 17.6 %all_gather.53 = bf16[768,640]{1,0:T(8,128)(2,1)} all-gather(bf16[96,640]{1,0:T(8,128)(2,1)S(1)} %slice-done.1), channel_id=1, replica_groups=mesh['dp'=4,'fsdp'=8] {'fsdp'}, dimensions={0}, use_global_device_ids=true | all-gather | bytes 1105920 | tf_op jit(solution)/shard_map/all_gather | solution.py:145
  132.2 17.6 %all_gather.51 = bf16[768,640]{1,0:T(8,128)(2,1)} all-gather(bf16[96,640]{1,0:T(8,128)(2,1)S(1)} %slice-done), channel_id=1, replica_groups=mesh['dp'=4,'fsdp'=8] {'fsdp'}, dimensions={0}, use_global_device_ids=true | all-gather | bytes 1105920 | tf_op jit(solution)/shard_map/all_gather | solution.py:144
  166.4 89.9 %while.28 = (s32[]{:T(128)}, bf16[2,640,640]{2,1,0:T(8,128)(2,1)}, f32[2,10,640,1]{2,1,3,0:T(8,128)S(1)}, bf16[2,640,10,64]{1,3,2,0:T(8,128)(2,1)}, bf16[1280,10...) while((s32[]{:T(128)}, bf16[2,640,640]{2,1,0:T(8,128)(2,1)}, ...), condition=%wide.region_3.4_spmd.clone, body=%wide.region_0.3_spmd.clone.sunk | while | flops 2154490880 | bytes 106764904 | solution.py:72
  167.6 14.5 %fusion.117 = (f32[10,640]{1,0:T(8,128)S(1)}, f32[10,640,1280]{2,1,0:T(8,128)}) fusion(bf16[1280,10,64]{0,2,1:T(8,128)(2,1)S(1)} %get-tuple-element.510, bf16[2,640,10,64]{1,3,2,0:T(8,128)(2,1)} %get-tuple-element.509, s32[]{:T(128)S(6)} %copy.158, pred[1280]{0:T(1024)(128)(4,1)S(1)} %compare_reduce_fusion.4), kind=kOutput, calls=%fused_computation.141.clone.1 | convolution fusion | flops 1073145600 | bytes 35252484 | tf_op jit(solution)/shard_map/while/body/eval_jaxpr/qhd,khd->hqk/dot_general | solution.py:28
  182.1 11.2 %exponential_reduce_fusion.2 = f32[10,640]{1,0:T(8,128)S(1)} fusion(f32[10,640,1280]{2,1,0:T(8,128)} %get-tuple-element.474, f32[10,640]{1,0:T(8,128)S(1)} %get-tuple-element.475), kind=kLoop, calls=%fused_computation.3.clone.1 | loop fusion | flops 16377600 | bytes 32819200 | tf_op jit(solution)/shard_map/while/body/eval_jaxpr/reduce_sum | solution.py:67
  193.4 13.9 %fusion.118 = bf16[10,640,64]{1,2,0:T(8,128)(2,1)} fusion(bf16[1280,10,64]{0,2,1:T(8,128)(2,1)S(1)} %get-tuple-element.511, f32[10,640,1280]{2,1,0:T(8,128)} %get-tuple-element.474, f32[10,640]{1,0:T(8,128)S(1)} %get-tuple-element.476), kind=kOutput, calls=%fused_computation.5.clone.1 | convolution fusion | flops 1064960000 | bytes 35251200 | tf_op jit(solution)/shard_map/while/body/eval_jaxpr/hqk,khd->qhd/dot_general | solution.py:28
  212.3 14.5 %fusion.117 = (f32[10,640]{1,0:T(8,128)S(1)}, f32[10,640,1280]{2,1,0:T(8,128)}) fusion(bf16[1280,10,64]{0,2,1:T(8,128)(2,1)S(1)} %get-tuple-element.510, bf16[2,640,10,64]{1,3,2,0:T(8,128)(2,1)} %get-tuple-element.509, s32[]{:T(128)S(6)} %copy.158, pred[1280]{0:T(1024)(128)(4,1)S(1)} %compare_reduce_fusion.4), kind=kOutput, calls=%fused_computation.141.clone.1 | convolution fusion | flops 1073145600 | bytes 35252484 | tf_op jit(solution)/shard_map/while/body/eval_jaxpr/qhd,khd->hqk/dot_general | solution.py:28
  226.8 11.2 %exponential_reduce_fusion.2 = f32[10,640]{1,0:T(8,128)S(1)} fusion(f32[10,640,1280]{2,1,0:T(8,128)} %get-tuple-element.474, f32[10,640]{1,0:T(8,128)S(1)} %get-tuple-element.475), kind=kLoop, calls=%fused_computation.3.clone.1 | loop fusion | flops 16377600 | bytes 32819200 | tf_op jit(solution)/shard_map/while/body/eval_jaxpr/reduce_sum | solution.py:67
  238.1 13.9 %fusion.118 = bf16[10,640,64]{1,2,0:T(8,128)(2,1)} fusion(bf16[1280,10,64]{0,2,1:T(8,128)(2,1)S(1)} %get-tuple-element.511, f32[10,640,1280]{2,1,0:T(8,128)} %get-tuple-element.474, f32[10,640]{1,0:T(8,128)S(1)} %get-tuple-element.476), kind=kOutput, calls=%fused_computation.5.clone.1 | convolution fusion | flops 1064960000 | bytes 35251200 | tf_op jit(solution)/shard_map/while/body/eval_jaxpr/hqk,khd->qhd/dot_general | solution.py:28
  262.4 36.7 %multiply_convert_fusion.1 = (bf16[1280,2240]{0,1:T(8,128)(2,1)}, f32[1280,2240]{0,1:T(8,128)}, f32[1280,2240]{0,1:T(8,128)}) fusion(f32[2240]{0:T(1024)S(1)} %copy-done.46, bf16[768,2240]{1,0:T(8,128)(2,1)} %all-gather.4.cloned.1.call-done, f32[1280,640]{0,1:T(8,128)} %copy-done.7, f32[640]{0:T(1024)S(1)} %get-tuple-element.373, f32[640]{0:T(1024)S(1)} %copy-done.40, ...), kind=kOutput, calls=%fused_computation.46 | convolution fusion | flops 3863347200 | bytes 34922240 | tf_op jit(solution)/shard_map/rw,wh->rh/dot_general | solution.py:28
  315.9 18.0 %convert_reduce_fusion = (f32[2240]{0:T(1024)}, bf16[1280,2240]{0,1:T(8,128)(2,1)}) fusion(f32[1280,2240]{0,1:T(8,128)} %get-tuple-element.354, f32[1280,2240]{0,1:T(8,128)} %get-tuple-element.366, bf16[1280,640]{0,1:T(8,128)(2,1)} %get-tuple-element.346, bf16[3072,640]{1,0:T(8,128)(2,1)} %all-gather.6.cloned.1.call-done), kind=kOutput, calls=%fused_computation.44 | convolution fusion | flops 3715888896 | bytes 33186560 | tf_op jit(solution)/shard_map/rw,hw->rh/dot_general | solution.py:28
  363.0 211.4 %while.29 = (s32[]{:T(128)}, f32[1280,10,64]{0,2,1:T(8,128)}, f32[1280,10,64]{0,2,1:T(8,128)}, bf16[2,640,640]{2,1,0:T(8,128)(2,1)}, bf16[2,640,10,64]{1,3,2,0:T...) while((s32[]{:T(128)}, f32[1280,10,64]{0,2,1:T(8,128)}, ...), condition=%wide.region_14.15_spmd.clone, body=%wide.region_12.14_spmd.clone.sunk | while | flops 5321518080 | bytes 363052608 | solution.py:101
  363.7 14.3 %fusion.128 = f32[10,640,1280]{2,1,0:T(8,128)} fusion(bf16[1280,10,64]{0,2,1:T(8,128)(2,1)S(1)} %get-tuple-element.546, bf16[2,640,10,64]{1,3,2,0:T(8,128)(2,1)} %get-tuple-element.545, s32[]{:T(128)S(6)} %copy.168), kind=kOutput, calls=%fused_computation.26.clone.1 | convolution fusion | flops 1048576000 | bytes 35225604 | tf_op jit(solution)/shard_map/while/body/eval_jaxpr/qhd,khd->hqk/dot_general | solution.py:28
  378.1 26.1 %multiply_reduce_fusion.8 = (f32[10,640]{1,0:T(8,128)S(1)}, f32[10,640,1280]{2,1,0:T(8,128)}) fusion(f32[10,640,1280]{2,1,0:T(8,128)} %fusion.128, f32[10,640]{1,0:T(8,128)S(1)} %dynamic-slice_bitcast_fusion.2, bf16[1280,10,64]{0,2,1:T(8,128)(2,1)S(1)} %get-tuple-element.543, bf16[2,640,10,64]{1,3,2,0:T(8,128)(2,1)S(1)} %copy-done.3, ...), kind=kOutput, calls=%fused_computation.15.clone.1 | convolution fusion | flops 1089529600 | bytes 68062208 | tf_op jit(solution)/shard_map/while/body/eval_jaxpr/qhd,khd->hqk/dot_general | solution.py:28
  404.2 27.0 %multiply_convert_fusion.4 = bf16[10,640,1280]{2,1,0:T(8,128)(2,1)} fusion(f32[10,640,1280]{2,1,0:T(8,128)} %get-tuple-element.488, f32[10,640,1280]{2,1,0:T(8,128)} %fusion.128, f32[10,640]{1,0:T(8,128)S(1)} %get-tuple-element.489), kind=kLoop, calls=%fused_computation.14.clone.1 | loop fusion | flops 24576000 | bytes 81945600 | tf_op jit(solution)/shard_map/while/body/eval_jaxpr/convert_element_type | solution.py:94
  431.2 15.0 %fusion.130 = f32[1280,10,64]{0,2,1:T(8,128)} fusion(f32[10,640,1280]{2,1,0:T(8,128)} %get-tuple-element.488, f32[1280,10,64]{0,2,1:T(8,128)} %get-tuple-element.528, pred[]{:T(512)S(6)} %compare.18, bf16[2,640,10,64]{1,3,2,0:T(8,128)(2,1)S(1)} %copy-done.5, s32[]{:T(128)S(6)} %copy.168), kind=kOutput, calls=%fused_computation.23.clone.1 | convolution fusion | flops 1058406400 | bytes 40140804 | tf_op jit(solution)/shard_map/while/body/eval_jaxpr/hqk,qhd->khd/dot_general | solution.py:28
  468.3 14.3 %fusion.128 = f32[10,640,1280]{2,1,0:T(8,128)} fusion(bf16[1280,10,64]{0,2,1:T(8,128)(2,1)S(1)} %get-tuple-element.546, bf16[2,640,10,64]{1,3,2,0:T(8,128)(2,1)} %get-tuple-element.545, s32[]{:T(128)S(6)} %copy.168), kind=kOutput, calls=%fused_computation.26.clone.1 | convolution fusion | flops 1048576000 | bytes 35225604 | tf_op jit(solution)/shard_map/while/body/eval_jaxpr/qhd,khd->hqk/dot_general | solution.py:28
  482.7 26.1 %multiply_reduce_fusion.8 = (f32[10,640]{1,0:T(8,128)S(1)}, f32[10,640,1280]{2,1,0:T(8,128)}) fusion(f32[10,640,1280]{2,1,0:T(8,128)} %fusion.128, f32[10,640]{1,0:T(8,128)S(1)} %dynamic-slice_bitcast_fusion.2, bf16[1280,10,64]{0,2,1:T(8,128)(2,1)S(1)} %get-tuple-element.543, bf16[2,640,10,64]{1,3,2,0:T(8,128)(2,1)S(1)} %copy-done.3, ...), kind=kOutput, calls=%fused_computation.15.clone.1 | convolution fusion | flops 1089529600 | bytes 68062208 | tf_op jit(solution)/shard_map/while/body/eval_jaxpr/qhd,khd->hqk/dot_general | solution.py:28
  508.8 27.0 %multiply_convert_fusion.4 = bf16[10,640,1280]{2,1,0:T(8,128)(2,1)} fusion(f32[10,640,1280]{2,1,0:T(8,128)} %get-tuple-element.488, f32[10,640,1280]{2,1,0:T(8,128)} %fusion.128, f32[10,640]{1,0:T(8,128)S(1)} %get-tuple-element.489), kind=kLoop, calls=%fused_computation.14.clone.1 | loop fusion | flops 24576000 | bytes 81945600 | tf_op jit(solution)/shard_map/while/body/eval_jaxpr/convert_element_type | solution.py:94
  535.8 15.9 %fusion.130 = f32[1280,10,64]{0,2,1:T(8,128)} fusion(f32[10,640,1280]{2,1,0:T(8,128)} %get-tuple-element.488, f32[1280,10,64]{0,2,1:T(8,128)} %get-tuple-element.528, pred[]{:T(512)S(6)} %compare.18, bf16[2,640,10,64]{1,3,2,0:T(8,128)(2,1)S(1)} %copy-done.5, s32[]{:T(128)S(6)} %copy.168), kind=kOutput, calls=%fused_computation.23.clone.1 | convolution fusion | flops 1058406400 | bytes 40140804 | tf_op jit(solution)/shard_map/while/body/eval_jaxpr/hqk,qhd->khd/dot_general | solution.py:28
  633.2 24.6 %reduce-scatter.15.cloned.1.call-done = f32[96,768]{1,0:T(8,128)} async-done(((f32[768,768]{1,0:T(8,128)}), f32[96,768]{1,0:T(8,128)}) %reduce-scatter.15.cloned.1.call-update) | async-done | bytes 294928 | tf_op jit(solution)/shard_map/reduce_scatter | solution.py:275
  659.5 36.2 %reduce-scatter.19.cloned.1.call-done = f32[96,768]{1,0:T(8,128)} async-done(((f32[768,768]{1,0:T(8,128)}), f32[96,768]{1,0:T(8,128)}) %reduce-scatter.19.cloned.1.call-update) | async-done | bytes 294928
  697.4 35.9 %reduce-scatter.23.cloned.1.call-done = f32[96,768]{1,0:T(8,128)} async-done(((f32[768,768]{1,0:T(8,128)}), f32[96,768]{1,0:T(8,128)}) %reduce-scatter.23.cloned.1.call-update) | async-done | bytes 294928
  735.0 99.4 %reduce-scatter.25.cloned.1.call-done = f32[96,3072]{1,0:T(8,128)} async-done(((f32[768,3072]{1,0:T(8,128)}), f32[96,3072]{1,0:T(8,128)}) %reduce-scatter.25.cloned.1.call-update) | async-done | bytes 1179664
  836.8 97.8 %reduce-scatter.17.cloned.1.call-done = f32[384,768]{1,0:T(8,128)} async-done(((f32[3072,768]{1,0:T(8,128)}), f32[384,768]{1,0:T(8,128)}) %reduce-scatter.17.cloned.1.call-update) | async-done | bytes 1179664 | tf_op jit(solution)/shard_map/reduce_scatter | solution.py:281
  951.4 26.4 %all-reduce.32 = (bf16[768]{0:T(1024)(128)(2,1)S(1)}, bf16[768]{0:T(1024)(128)(2,1)S(1)}, bf16[768]{0:T(1024)(128)(2,1)S(1)}, bf16[3072]{0:T(1024)(128)(2,1)S(1)...) all-reduce(f32[768]{0:T(1024)S(1)} %pad.56, ...), channel_id=8, replica_groups=mesh['dp'=4,'fsdp'=8] {'fsdp'}, use_global_device_ids=true, to_apply=%region_28.29.clone | all-reduce | flops 9216 | bytes 55296
  978.5 10.1 all-reduce.34
  993.3 15.5 %all-reduce.38.cloned.1.call-done = (bf16[96,768]{0,1:T(8,128)(2,1)}, bf16[96,768]{0,1:T(8,128)(2,1)}, bf16[96,768]{0,1:T(8,128)(2,1)}, bf16[96,3072]{0,1:T(8,12...) async-done(((bf16[96,768]{0,1:T(8,128)(2,1)}, bf16[96,768]{0,1:T(8,128)(2,1)}, bf16[96,768]{0,1:T(8,128)(2,1)}, bf16[96,3072]{0,1:T(8,128)(2,1)}, ...) | async-done | bytes 1769488 | tf_op jit(solution)/shard_map/psum | solution.py:313
  (296 shorter events, 237.3 us)
Async XLA Ops:
  7.2 107.4 %slice-start.1 = ((bf16[96,768]{1,0:T(8,128)(2,1)}), bf16[96,640]{1,0:T(8,128)(2,1)S(1)}, s32[]{:S(2)}) async-start(bf16[96,768]{1,0:T(8,128)(2,1)} %param.25), calls=%async_computation.16 | async-start | bytes 245760 | tf_op jit(solution)/shard_map/slice | solution.py:145
  7.2 85.0 %slice-start.2 = ((bf16[96,768]{1,0:T(8,128)(2,1)}), bf16[96,640]{1,0:T(8,128)(2,1)S(1)}, s32[]{:S(2)}) async-start(bf16[96,768]{1,0:T(8,128)(2,1)} %param.26), calls=%async_computation.17 | async-start | bytes 245760 | tf_op jit(solution)/shard_map/slice | solution.py:146
  7.2 62.6 %slice-start.3 = ((bf16[96,768]{1,0:T(8,128)(2,1)}), bf16[96,640]{1,0:T(8,128)(2,1)S(1)}, s32[]{:S(2)}) async-start(bf16[96,768]{1,0:T(8,128)(2,1)} %param.27), calls=%async_computation.18 | async-start | bytes 245760 | tf_op jit(solution)/shard_map/slice | solution.py:147
  7.2 255.1 %all-gather.4.cloned.1.call-start = ((), (), s32[]{:S(2)}) async-start(), calls=%async_computation.6 | async-start | bytes 3981312 | tf_op jit(solution)/shard_map/all_gather | solution.py:148
  9.2 123.0 %slice-start = ((bf16[96,768]{1,0:T(8,128)(2,1)}), bf16[96,640]{1,0:T(8,128)(2,1)S(1)}, s32[]{:S(2)}) async-start(bf16[96,768]{1,0:T(8,128)(2,1)} %param.24), calls=%async_computation.15 | async-start | bytes 245760 | tf_op jit(solution)/shard_map/slice | solution.py:144
  9.2 289.8 %all-gather.6.cloned.1.call-start = ((), (), s32[]{:S(2)}) async-start(), calls=%async_computation.7 | async-start | bytes 4423680 | tf_op jit(solution)/shard_map/all_gather | solution.py:149
  11.1 138.7 %copy-start.20 = (bf16[1280,640]{1,0:T(8,128)(2,1)S(1)}, bf16[1280,640]{1,0:T(8,128)(2,1)}, u32[]{:S(2)}) copy-start(bf16[1280,640]{1,0:T(8,128)(2,1)} %param.22) | copy-start | bytes 4915204
  11.2 620.3 %reduce-scatter.21.cloned.1.call-start = ((), (), s32[]{:S(2)}) async-start(), calls=%async_computation.11 | async-start | bytes 2654208
  166.4 89.9 %copy-start.50 = (f32[640]{0:T(1024)S(1)}, f32[640]{0:T(1024)}, u32[]{:S(2)}) copy-start(f32[640]{0:T(1024)} %slice_convert_fusion.6) | copy-start | bytes 7684
  260.2 82.9 %copy-start.32 = (f32[1280]{0:T(1024)}, f32[1280]{0:T(1024)S(1)}, u32[]{:S(2)}) copy-start(f32[1280]{0:T(1024)S(1)} %broadcast_multiply_fusion.1) | copy-start | bytes 15364
  262.3 80.9 %copy-start.36 = (f32[1280]{0:T(1024)}, f32[1280]{0:T(1024)S(1)}, u32[]{:S(2)}) copy-start(f32[1280]{0:T(1024)S(1)} %fusion.58) | copy-start | bytes 15364
  262.3 36.8 %copy-start.47 = (f32[640]{0:T(1024)}, f32[640]{0:T(1024)S(1)}, u32[]{:S(2)}) copy-start(f32[640]{0:T(1024)S(1)} %get-tuple-element.373) | copy-start | bytes 7684
  262.4 36.7 %copy-start.49 = (f32[640]{0:T(1024)S(1)}, f32[640]{0:T(1024)}, u32[]{:S(2)}) copy-start(f32[640]{0:T(1024)} %slice_convert_fusion.3) | copy-start | bytes 7684
  299.1 9.0 copy-start.6
  315.9 18.0 %copy-start.8 = (f32[1280,640]{0,1:T(8,128)S(1)}, f32[1280,640]{0,1:T(8,128)}, u32[]{:S(2)}) copy-start(f32[1280,640]{0,1:T(8,128)} %copy-done.7) | copy-start | bytes 9830404
  363.0 15.0 %copy-start.1 = (bf16[1280,10,64]{0,2,1:T(8,128)(2,1)}, bf16[1280,10,64]{0,2,1:T(8,128)(2,1)S(1)}, u32[]{:S(2)}) copy-start(bf16[1280,10,64]{0,2,1:T(8,128)(2,1)S(1)} %get-tuple-element.543) | copy-start | bytes 4915204 | tf_op jit(solution)/shard_map/while
  363.7 14.4 %copy-start.3 = (bf16[2,640,10,64]{1,3,2,0:T(8,128)(2,1)S(1)}, bf16[2,640,10,64]{1,3,2,0:T(8,128)(2,1)}, u32[]{:S(2)}) copy-start(bf16[2,640,10,64]{1,3,2,0:T(8,128)(2,1)} %get-tuple-element.542) | copy-start | bytes 4915204 | tf_op jit(solution)/shard_map/while
  404.2 27.0 %copy-start.5 = (bf16[2,640,10,64]{1,3,2,0:T(8,128)(2,1)S(1)}, bf16[2,640,10,64]{1,3,2,0:T(8,128)(2,1)}, u32[]{:S(2)}) copy-start(bf16[2,640,10,64]{1,3,2,0:T(8,128)(2,1)} %get-tuple-element.545) | copy-start | bytes 4915204 | tf_op jit(solution)/shard_map/while
  446.2 11.1 %copy-start = (bf16[10,640,1280]{2,1,0:T(8,128)(2,1)S(1)}, bf16[10,640,1280]{2,1,0:T(8,128)(2,1)}, u32[]{:S(2)}) copy-start(bf16[10,640,1280]{2,1,0:T(8,128)(2,1)} %multiply_convert_fusion.4) | copy-start | bytes 49152004 | tf_op jit(solution)/shard_map/while
  467.6 15.0 %copy-start.1 = (bf16[1280,10,64]{0,2,1:T(8,128)(2,1)}, bf16[1280,10,64]{0,2,1:T(8,128)(2,1)S(1)}, u32[]{:S(2)}) copy-start(bf16[1280,10,64]{0,2,1:T(8,128)(2,1)S(1)} %get-tuple-element.543) | copy-start | bytes 4915204 | tf_op jit(solution)/shard_map/while
  468.3 14.4 %copy-start.3 = (bf16[2,640,10,64]{1,3,2,0:T(8,128)(2,1)S(1)}, bf16[2,640,10,64]{1,3,2,0:T(8,128)(2,1)}, u32[]{:S(2)}) copy-start(bf16[2,640,10,64]{1,3,2,0:T(8,128)(2,1)} %get-tuple-element.542) | copy-start | bytes 4915204 | tf_op jit(solution)/shard_map/while
  508.8 27.0 %copy-start.5 = (bf16[2,640,10,64]{1,3,2,0:T(8,128)(2,1)S(1)}, bf16[2,640,10,64]{1,3,2,0:T(8,128)(2,1)}, u32[]{:S(2)}) copy-start(bf16[2,640,10,64]{1,3,2,0:T(8,128)(2,1)} %get-tuple-element.545) | copy-start | bytes 4915204 | tf_op jit(solution)/shard_map/while
  551.7 11.1 %copy-start = (bf16[10,640,1280]{2,1,0:T(8,128)(2,1)S(1)}, bf16[10,640,1280]{2,1,0:T(8,128)(2,1)}, u32[]{:S(2)}) copy-start(bf16[10,640,1280]{2,1,0:T(8,128)(2,1)} %multiply_convert_fusion.4) | copy-start | bytes 49152004 | tf_op jit(solution)/shard_map/while
  584.1 73.7 %reduce-scatter.15.cloned.1.call-start = ((), (), s32[]{:S(2)}) async-start(), calls=%async_computation.8 | async-start | bytes 2654208 | tf_op jit(solution)/shard_map/reduce_scatter | solution.py:275
  589.2 106.5 %reduce-scatter.19.cloned.1.call-start = ((), (), s32[]{:S(2)}) async-start(), calls=%async_computation.10 | async-start | bytes 2654208
  598.4 134.9 %reduce-scatter.23.cloned.1.call-start = ((), (), s32[]{:S(2)}) async-start(), calls=%async_computation.12 | async-start | bytes 2654208
  606.8 227.6 %reduce-scatter.25.cloned.1.call-start = ((), (), s32[]{:S(2)}) async-start(), calls=%async_computation.13 | async-start | bytes 10616832
  618.7 315.9 %reduce-scatter.17.cloned.1.call-start = ((), (), s32[]{:S(2)}) async-start(), calls=%async_computation.9 | async-start | bytes 10616832 | tf_op jit(solution)/shard_map/reduce_scatter | solution.py:281
  631.4 377.4 %all-reduce.38.cloned.1.call-start = ((), (), s32[]{:S(2)}) async-start(), calls=%async_computation.14 | async-start | bytes 4227072 | tf_op jit(solution)/shard_map/psum | solution.py:313
  836.8 104.8 %copy-start.11 = (f32[1280,640]{0,1:T(8,128)S(1)}, f32[1280,640]{0,1:T(8,128)}, u32[]{:S(2)}) copy-start(f32[1280,640]{0,1:T(8,128)} %copy-done.10) | copy-start | bytes 9830404
  836.8 104.8 %copy-start.35 = (f32[1280]{0:T(1024)S(1)}, f32[1280]{0:T(1024)}, u32[]{:S(2)}) copy-start(f32[1280]{0:T(1024)} %copy-done.34) | copy-start | bytes 15364
  1008.8 9.4 copy-start.30
  (41 other events, 114.5 us)
Sparse Core Ops, SparseCore 0:
  9.7 44.8 all-gather.3
  56.2 59.4 all-gather.5
  584.2 35.8 reduce-scatter.20
  622.4 35.4 reduce-scatter.14
  660.0 35.5 reduce-scatter.18
  697.8 35.4 reduce-scatter.22
  735.6 98.7 reduce-scatter.24
  836.7 97.8 reduce-scatter.16
  939.0 69.7 all-reduce.37
where the time goes:
time: 1040 us; the launch traced here: 1030 us
  matrix products  319 us (31%)
  waiting for transfers between devices  309 us (30%)
  blocking collectives  161 us (15%)
  local copies, waits for them, and re-layouts  110 us (11%)
  other arithmetic  107 us (10%)
  between operations  17.9 us (2%)
    dot_general x31, matrix products, matmul(): jnp.einsum(pattern, left_side, right_side, preferred_element_type=jnp.flo...  313 us
    unnamed x13, waiting for transfers between devices  172 us
    reduce_scatter x1, waiting for transfers between devices, on_device(): lax.psum_scatter(widen(down_term, SUPER_HIDDEN, column_count), 'fsdp', sc...  97.8 us
    unnamed x2, blocking collectives  58.5 us
    unnamed x145, local copies, waits for them, and re-layouts  56 us
    convert_element_type x2, other arithmetic, one_block(): grad_scores = (prob_full * (grad_probs - weighted)).astype(jnp.bfloat16)  54 us
    reduce_scatter x1, waiting for transfers between devices, on_device(): lax.psum_scatter(widen(out_term, SUPER_WIDTH, column_count), 'fsdp', scat...  24.6 us
    reduce_sum x2, other arithmetic, one_block(): jnp.sum(jnp.exp(scores - highest), -1, keepdims=True)  22.5 us
  transfers between devices with their start and end apart: 9, of which 6 were waited for; matrix products, arithmetic and copies ran while one was open for 23% of the time, Pallas kernels for 0%

commit v1 on v0

v1 whole, which is shorter than its diff:
```python
import functools

import jax
import jax.numpy as jnp
from jax import lax
from jax.experimental import pallas as pl
from jax.experimental.pallas import tpu as pltpu
from jax.sharding import PartitionSpec as P

HEAD_DIM = 64
HIDDEN_SIZE = 2240
WIDTH = 640
EPSILON = 1e-05
MASKED = -1e30
PAIR = 2 * HEAD_DIM
PAIRS = WIDTH // PAIR
BF = jnp.bfloat16
F32 = jnp.float32
VMEM_BYTES = 60 * 2**20


def dot(left, right, left_dim, right_dim):
    return lax.dot_general(
        left, right, (((left_dim,), (right_dim,)), ((), ())), preferred_element_type=F32
    )


def side(shape, axis, half, own, flag):
    place = lax.broadcasted_iota(jnp.int32, shape, axis)
    mine = (place < HEAD_DIM) if half == 0 else (place >= HEAD_DIM)
    first = place == (HEAD_DIM if half == 0 else 0)
    return jnp.where(mine, own, jnp.where(first, flag, 0.0))


def attend_kernel(
    length_ref, token_ref, wq_ref, wk_ref, wv_ref, bq_ref, bv_ref,
    exp_ref, context_ref, wide_ref, inverse_ref, query_t_ref, key_ref, value_t_ref,
):
    rows = token_ref.shape[0]
    weights = jnp.concatenate([wq_ref[...], wk_ref[...], wv_ref[...]], axis=1)
    product = dot(token_ref[...], weights, 1, 0)
    query = (product[:, :PAIR] + bq_ref[...]).astype(BF)
    key = product[:, PAIR : 2 * PAIR].astype(BF)
    value = (product[:, 2 * PAIR :] + bv_ref[...]).astype(BF)
    key_t = key.T
    query_t_ref[...] = query.T
    key_ref[...] = key
    value_t_ref[...] = value.T
    key_place = lax.broadcasted_iota(jnp.int32, (1, rows), 1)
    bias = jnp.where(key_place < length_ref[0], 0.0, MASKED)
    scaled = query.astype(F32) * HEAD_DIM**-0.5
    key_wide = key_t.astype(F32)
    value_wide = value.astype(F32)
    block = 128
    results = []
    for half in range(2):
        left = side((rows, PAIR), 1, half, scaled, 1.0).astype(BF)
        place = lax.broadcasted_iota(jnp.int32, (PAIR, rows), 0)
        right = jnp.where(place == (HEAD_DIM if half == 0 else 0), bias, key_wide).astype(BF)
        for start in range(0, rows, block):
            scores = dot(left[start : start + block], right, 1, 0)
            highest = jnp.max(scores, 1, keepdims=True)
            exp_ref[half, start : start + block, :] = jnp.exp(scores - highest).astype(BF)
        values = side((rows, PAIR), 1, half, value_wide, 1.0).astype(BF)
        total = dot(exp_ref[half], values, 1, 0)
        flag = HEAD_DIM if half == 0 else 0
        inverse = 1.0 / total[:, flag : flag + 1]
        results.append((total * inverse, inverse))
    low = lax.broadcasted_iota(jnp.int32, (rows, PAIR), 1) < HEAD_DIM
    context = jnp.where(low, results[0][0], results[1][0])
    wide_ref[...] = context
    context_ref[...] = context.astype(BF)
    inverse_ref[...] = jnp.where(low, results[0][1], results[1][1])


def attend(tokens, lengths, wide_weights, vectors):
    rows = tokens.shape[0]
    column = lambda first: pl.BlockSpec((WIDTH, PAIR), lambda p: (0, first + p))
    vector = lambda: pl.BlockSpec((1, PAIR), lambda p: (0, p))
    tall = lambda: pl.BlockSpec((rows, PAIR), lambda p: (0, p))
    flat = lambda: pl.BlockSpec((PAIR, rows), lambda p: (p, 0))
    return pl.pallas_call(
        attend_kernel,
        grid=(PAIRS,),
        in_specs=[
            pl.BlockSpec(memory_space=pltpu.SMEM),
            pl.BlockSpec((rows, WIDTH), lambda p: (0, 0)),
            column(0), column(PAIRS), column(2 * PAIRS),
            vector(), vector(),
        ],
        out_specs=[
            pl.BlockSpec((2, rows, rows), lambda p: (p, 0, 0)),
            tall(), tall(), tall(), flat(), tall(), flat(),
        ],
        out_shape=[
            jax.ShapeDtypeStruct((2 * PAIRS, rows, rows), BF),
            jax.ShapeDtypeStruct((rows, WIDTH), BF),
            jax.ShapeDtypeStruct((rows, WIDTH), F32),
            jax.ShapeDtypeStruct((rows, WIDTH), F32),
            jax.ShapeDtypeStruct((WIDTH, rows), BF),
            jax.ShapeDtypeStruct((rows, WIDTH), BF),
            jax.ShapeDtypeStruct((WIDTH, rows), BF),
        ],
        compiler_params=pltpu.CompilerParams(vmem_limit_bytes=VMEM_BYTES),
    )(lengths, tokens, wide_weights, wide_weights, wide_weights, vectors[0:1], vectors[1:2])


def gelu_pair(values):
    t = 1.0 / (1.0 + (0.3275911 * 0.5**0.5) * jnp.abs(values))
    bell = jnp.exp(-0.5 * values * values)
    tail = t * (0.5 * 0.254829592 + t * (0.5 * -0.284496736 + t * (0.5 * 1.421413741 + t * (
        0.5 * -1.453152027 + t * (0.5 * 1.061405429)))))
    tail = tail * bell
    share = jnp.where(values >= 0.0, 1.0 - tail, tail)
    return values * share, share + values * bell * 0.3989422804014327


def row_mean(values):
    return jnp.sum(values, 1, keepdims=True) * (1.0 / WIDTH)


def column_sum(values):
    return jnp.sum(values, 0, keepdims=True)


def feed_kernel(
    length_ref, context_ref, token_ref, cotangent_ref, wo_ref, w1_ref, w2_ref, vector_ref, b1_ref,
    output_ref, normed_ref, active_ref, hidden_ref, feed_ref, first_ref, grad_context_ref,
    sums_ref, b1_sum_ref,
):
    step = pl.program_id(0)
    rows = token_ref.shape[0]
    place = lax.broadcasted_iota(jnp.int32, (rows, 1), 0) + step * rows
    live = jnp.where(place < length_ref[0], 1.0, 0.0)
    vector = lambda i: vector_ref[i : i + 1, :]
    out_add, down_add = vector(2), vector(3)
    gain_one, shift_one, gain_two, shift_two = vector(4), vector(5), vector(6), vector(7)
    first_sum = token_ref[...].astype(F32) + dot(context_ref[...], wo_ref[...], 1, 0) + out_add
    center = first_sum - row_mean(first_sum)
    rate_one = lax.rsqrt(row_mean(center * center) + EPSILON)
    unit_one = center * rate_one
    normed = (unit_one * gain_one + shift_one).astype(BF)
    normed_ref[...] = normed
    pre = dot(normed, w1_ref[...], 1, 0) + b1_ref[...]
    active_full, slope = gelu_pair(pre)
    active = active_full.astype(BF)
    active_ref[...] = active
    second_sum = normed.astype(F32) + dot(active, w2_ref[...], 1, 0) + down_add
    center = second_sum - row_mean(second_sum)
    rate_two = lax.rsqrt(row_mean(center * center) + EPSILON)
    unit_two = center * rate_two
    output_ref[...] = ((unit_two * gain_two + shift_two) * live).astype(BF)
    cotangent = cotangent_ref[...].astype(F32) * live
    inner = cotangent * gain_two
    grad_second = rate_two * (inner - row_mean(inner) - unit_two * row_mean(inner * unit_two))
    grad_feed = grad_second.astype(BF)
    feed_ref[...] = grad_feed
    grad_hidden = (dot(grad_feed, w2_ref[...], 1, 1) * slope).astype(BF)
    hidden_ref[...] = grad_hidden
    grad_normed = grad_second + dot(grad_hidden, w1_ref[...], 1, 1)
    inner = grad_normed * gain_one
    grad_first = rate_one * (inner - row_mean(inner) - unit_one * row_mean(inner * unit_one))
    first_ref[...] = grad_first
    grad_branch = grad_first.astype(BF)
    grad_context_ref[...] = dot(grad_branch, wo_ref[...], 1, 1).astype(BF)
    sums = jnp.concatenate(
        [
            column_sum(grad_branch.astype(F32)),
            column_sum(grad_feed.astype(F32)),
            column_sum(grad_normed * unit_one),
            column_sum(grad_normed),
            column_sum(cotangent * unit_two),
            column_sum(cotangent),
            jnp.zeros((2, WIDTH), F32),
        ],
        axis=0,
    )
    b1_sum = column_sum(grad_hidden.astype(F32))

    @pl.when(step == 0)
    def _():
        sums_ref[...] = sums
        b1_sum_ref[...] = b1_sum

    @pl.when(step > 0)
    def _():
        sums_ref[...] += sums
        b1_sum_ref[...] += b1_sum


def feed(lengths, context, tokens, cotangent, wo, w1, w2, vectors, b1):
    rows = tokens.shape[0]
    tile = 256
    part = lambda width: pl.BlockSpec((tile, width), lambda i: (i, 0))
    whole = lambda *shape: pl.BlockSpec(shape, lambda i: (0, 0))
    array = lambda width, kind: jax.ShapeDtypeStruct((rows, width), kind)
    return pl.pallas_call(
        feed_kernel,
        grid=(rows // tile,),
        in_specs=[
            pl.BlockSpec(memory_space=pltpu.SMEM),
            part(WIDTH), part(WIDTH), part(WIDTH),
            whole(WIDTH, WIDTH), whole(WIDTH, HIDDEN_SIZE), whole(HIDDEN_SIZE, WIDTH),
            whole(8, WIDTH), whole(1, HIDDEN_SIZE),
        ],
        out_specs=[
            part(WIDTH), part(WIDTH), part(HIDDEN_SIZE), part(HIDDEN_SIZE), part(WIDTH),
            part(WIDTH), part(WIDTH), whole(8, WIDTH), whole(1, HIDDEN_SIZE),
        ],
        out_shape=[
            array(WIDTH, BF), array(WIDTH, BF), array(HIDDEN_SIZE, BF), array(HIDDEN_SIZE, BF),
            array(WIDTH, BF), array(WIDTH, F32), array(WIDTH, BF),
            jax.ShapeDtypeStruct((8, WIDTH), F32),
            jax.ShapeDtypeStruct((1, HIDDEN_SIZE), F32),
        ],
        compiler_params=pltpu.CompilerParams(vmem_limit_bytes=VMEM_BYTES),
    )(lengths, context, tokens, cotangent, wo, w1, w2, vectors, b1)


def attend_back_kernel(
    grad_ref, wide_ref, inverse_ref, exp_ref, query_t_ref, key_ref, value_t_ref,
    dq_ref, dk_ref, dv_ref, sums_ref, score_ref,
):
    rows = grad_ref.shape[0]
    inverse = inverse_ref[...]
    grad = grad_ref[...].astype(F32)
    scaled = grad * inverse
    dots = scaled * wide_ref[...]
    scaled_t = scaled.T.astype(BF)
    value_wide = value_t_ref[...].astype(F32)
    lane = lax.broadcasted_iota(jnp.int32, (rows, PAIR), 1)
    place = lax.broadcasted_iota(jnp.int32, (PAIR, rows), 0)
    block = 128
    dq, dk_t, dv_t = [], [], []
    for half in range(2):
        mine = (lane < HEAD_DIM) if half == 0 else (lane >= HEAD_DIM)
        flag = HEAD_DIM if half == 0 else 0
        offset = jnp.sum(jnp.where(mine, -dots, 0.0), 1, keepdims=True)
        high = offset.astype(BF).astype(F32)
        rest = offset - high
        left = jnp.where(
            mine, scaled, jnp.where(lane == flag, high, jnp.where(lane == flag + 1, rest, 0.0))
        ).astype(BF)
        right = jnp.where((place == flag) | (place == flag + 1), 1.0, value_wide).astype(BF)
        for start in range(0, rows, block):
            grad_probs = dot(left[start : start + block], right, 1, 0)
            weight = exp_ref[half, start : start + block, :].astype(F32)
            score_ref[half, start : start + block, :] = (grad_probs * weight).astype(BF)
        own = slice(half * HEAD_DIM, (half + 1) * HEAD_DIM)
        dv_t.append(dot(scaled_t[own], exp_ref[half], 1, 0))
        dk_t.append(dot(query_t_ref[own, :], score_ref[half], 1, 0))
        dq.append(dot(score_ref[half], key_ref[...], 1, 0))
    factor = HEAD_DIM**-0.5
    dq_low = (jnp.where(lane < HEAD_DIM, dq[0], dq[1]) * factor).astype(BF)
    dk_low = (jnp.concatenate(dk_t, axis=0) * factor).T.astype(BF)
    dv_low = jnp.concatenate(dv_t, axis=0).T.astype(BF)
    dq_ref[...] = dq_low
    dk_ref[...] = dk_low
    dv_ref[...] = dv_low
    sums_ref[...] = jnp.concatenate(
        [
            column_sum(dq_low.astype(F32)),
            column_sum(dv_low.astype(F32)),
            jnp.zeros((6, PAIR), F32),
        ],
        axis=0,
    )


def attend_back(grad_context, wide, inverse, exps, query_t, key, value_t):
    rows = grad_context.shape[0]
    tall = lambda: pl.BlockSpec((rows, PAIR), lambda p: (0, p))
    flat = lambda: pl.BlockSpec((PAIR, rows), lambda p: (p, 0))
    return pl.pallas_call(
        attend_back_kernel,
        grid=(PAIRS,),
        in_specs=[
            tall(), tall(), tall(),
            pl.BlockSpec((2, rows, rows), lambda p: (p, 0, 0)),
            flat(), tall(), flat(),
        ],
        out_specs=[tall(), tall(), tall(), pl.BlockSpec((8, PAIR), lambda p: (0, p))],
        out_shape=[
            jax.ShapeDtypeStruct((rows, WIDTH), BF),
            jax.ShapeDtypeStruct((rows, WIDTH), BF),
            jax.ShapeDtypeStruct((rows, WIDTH), BF),
            jax.ShapeDtypeStruct((8, WIDTH), F32),
        ],
        scratch_shapes=[pltpu.VMEM((2, rows, rows), BF)],
        compiler_params=pltpu.CompilerParams(vmem_limit_bytes=VMEM_BYTES),
    )(grad_context, wide, inverse, exps, query_t, key, value_t)


def widen(matrix, row_count, column_count):
    return jnp.pad(matrix, ((0, row_count - matrix.shape[0]), (0, column_count - matrix.shape[1])))


def on_device(
    tokens, lengths, query_weight, key_weight, value_weight, out_weight, up_weight, down_weight,
    query_bias, value_bias, out_bias, up_bias, down_bias, first_gain, first_shift, second_gain,
    second_shift, cotangent,
):
    owned, super_width = query_weight.shape
    super_hidden = up_weight.shape[1]
    ratio = super_hidden // super_width
    gather = lambda part: lax.all_gather(part, "fsdp", axis=0, tiled=True)
    small = jnp.stack(
        [
            query_bias, value_bias, out_bias, down_bias,
            first_gain, first_shift, second_gain, second_shift,
        ],
        axis=1,
    )
    small = jnp.concatenate([small, up_bias.reshape(owned, ratio)], axis=1)
    small = widen(small, owned, 128)
    local = jnp.concatenate(
        [query_weight[:, :WIDTH], key_weight[:, :WIDTH], value_weight[:, :WIDTH], small], axis=1
    )
    first_chunk = gather(local)
    out_sub = gather(out_weight[:, :WIDTH])
    up_sub = gather(up_weight[:, :HIDDEN_SIZE])
    down_sub = gather(down_weight[:, :WIDTH])
    base = 3 * WIDTH
    vectors = first_chunk[:WIDTH, base : base + 8].astype(F32).T
    up_row = first_chunk[:, base + 8 : base + 8 + ratio].astype(F32).reshape(1, super_hidden)
    up_row = up_row[:, :HIDDEN_SIZE]

    exps, context, wide, inverse, query_t, key, value_t = attend(
        tokens, lengths, first_chunk, vectors
    )
    output, normed, active, grad_hidden, grad_feed, grad_first, grad_context, sums, up_sum = feed(
        lengths, context, tokens, cotangent, out_sub, up_sub, down_sub, vectors, up_row
    )
    grad_queries, grad_keys, grad_values, pair_sums = attend_back(
        grad_context, wide, inverse, exps, query_t, key, value_t
    )
    token_grad = (
        grad_first
        + dot(grad_queries, first_chunk[:WIDTH, :WIDTH], 1, 1)
        + dot(grad_keys, first_chunk[:WIDTH, WIDTH : 2 * WIDTH], 1, 1)
        + dot(grad_values, first_chunk[:WIDTH, 2 * WIDTH : base], 1, 1)
    ).astype(BF)
    term = lambda left, right: dot(left, right, 0, 0).astype(BF)
    scatter = lambda part: lax.psum_scatter(part, "fsdp", scatter_dimension=0, tiled=True)
    up_wide = jnp.pad(up_sum[0], (0, super_hidden - HIDDEN_SIZE)).reshape(super_width, ratio)
    small_terms = jnp.concatenate(
        [
            widen(jnp.concatenate([sums[:6], pair_sums[:2]], axis=0), 8, super_width).T,
            up_wide,
        ],
        axis=1,
    )
    small_terms = widen(small_terms, super_width, 128).astype(BF)
    qkv_terms = jnp.concatenate(
        [term(tokens, grad_queries), term(tokens, grad_keys), term(tokens, grad_values)], axis=1
    )
    summed = (
        scatter(
            jnp.concatenate([widen(qkv_terms, super_width, 3 * WIDTH), small_terms], axis=1)
        ),
        scatter(widen(term(context, grad_first.astype(BF)), super_width, WIDTH)),
        scatter(widen(term(normed, grad_hidden), super_width, HIDDEN_SIZE)),
        scatter(widen(term(active, grad_feed), super_hidden, WIDTH)),
    )
    first, out_total, up_total, down_total = [
        lax.psum(part, "dp").astype(F32) for part in summed
    ]
    full = lambda part: widen(part, part.shape[0], super_width)
    vector = lambda i: first[:, base + i]
    return (
        output,
        token_grad,
        full(first[:, :WIDTH]),
        full(first[:, WIDTH : 2 * WIDTH]),
        full(first[:, 2 * WIDTH : base]),
        full(out_total),
        widen(up_total, owned, super_hidden),
        full(down_total),
        vector(6),
        vector(7),
        vector(0),
        first[:, base + 8 : base + 8 + ratio].reshape(-1),
        vector(1),
        vector(2),
        vector(3),
        vector(4),
        vector(5),
    )


def solution(mesh):
    rows = P(("dp", "fsdp"), None)
    held = P("fsdp", None)
    line = P("fsdp")
    return jax.shard_map(
        on_device,
        mesh=mesh,
        in_specs=(rows, P(("dp", "fsdp"))) + (held,) * 6 + (line,) * 9 + (rows,),
        out_specs=(rows, rows) + (held,) * 6 + (line,) * 9,
        check_vma=False,
    )
```

time: 1040 us -> 497 us (0.48)
  matrix products: 319 us -> 36.3 us
  blocking collectives: 161 us -> 24 us
  Pallas kernels: 0 us -> 112 us
  other arithmetic: 107 us -> 7.09 us
  local copies, waits for them, and re-layouts: 110 us -> 43.5 us
  waiting for transfers between devices: 309 us -> 251 us
    dot_general x31 -> x9, matrix products: 313 us -> 36.3 us  [dot(): lax.dot_general(left, right, (((left_dim,), (right_dim,)), ((), ())), pre...]
    unnamed x13 -> x10, waiting for transfers between devices: 172 us -> 47.9 us
    pallas_call x0 -> x3, Pallas kernels: none -> 112 us  [the longest x1 39.7 us: feed(): pl.pallas_call(feed_kernel, grid=(rows // tile,), in_specs=[pl.BlockSpec(...]
    convert_element_type x25 -> x1, other arithmetic: 71 us -> 1.17 us  [on_device(): lax.psum(part, 'dp').astype(F32)]
    all_gather x5 -> x1, blocking collectives: 92.8 us -> 24 us  [on_device(): gather = lambda part: lax.all_gather(part, 'fsdp', axis=0, tiled=True)]
    all_gather x2 -> x3, waiting for transfers between devices: 0.04 us -> 66 us  [on_device(): gather = lambda part: lax.all_gather(part, 'fsdp', axis=0, tiled=True)]
    unnamed x2 -> x0, blocking collectives: 58.5 us -> none
    reduce_scatter x2, waiting for transfers between devices: 122 us -> 79.5 us  [on_device(): lax.psum_scatter(part, 'fsdp', scatter_dimension=0, tiled=True)]
  transfers between devices with their start and end apart: 9 -> 8, of which waited for: 6 -> 8; matrix products, arithmetic and copies ran while one was open for 23% -> 10% of each run, Pallas kernels for 0% -> 8%
where the time goes in v1:
time: 497 us; the launch traced here: 490 us
  waiting for transfers between devices  251 us (51%)
  Pallas kernels  112 us (23%)
  local copies, waits for them, and re-layouts  43.5 us (9%)
  matrix products  36.3 us (7%)
  blocking collectives  24 us (5%)
  between operations  15.6 us (3%)
  other arithmetic  7.09 us (1%)
    reduce_scatter x2, waiting for transfers between devices, on_device(): lax.psum_scatter(part, 'fsdp', scatter_dimension=0, tiled=True)  79.5 us
    all_gather x3, waiting for transfers between devices, on_device(): gather = lambda part: lax.all_gather(part, 'fsdp', axis=0, tiled=True)  66 us
    psum x1, waiting for transfers between devices, on_device(): lax.psum(part, 'dp').astype(F32)  57.6 us
    unnamed x10, waiting for transfers between devices  47.9 us
    pallas_call x1, Pallas kernels, feed(): pl.pallas_call(feed_kernel, grid=(rows // tile,), in_specs=[pl.BlockSpec(...  39.7 us
    pallas_call x1, Pallas kernels, attend(): pl.pallas_call(attend_kernel, grid=(PAIRS,), in_specs=[pl.BlockSpec(memor...  38.4 us
    dot_general x9, matrix products, dot(): lax.dot_general(left, right, (((left_dim,), (right_dim,)), ((), ())), pre...  36.3 us
    pallas_call x1, Pallas kernels, attend_back(): pl.pallas_call(attend_back_kernel, grid=(PAIRS,), in_specs=[tall(), tall(...  33.8 us
  transfers between devices with their start and end apart: 8, of which 8 were waited for; matrix products, arithmetic and copies ran while one was open for 10% of the time, Pallas kernels for 8%

profile of v1, /device:TPU:0, one launch (start us, length us, event | category | flops | bytes accessed | tf_op | source)
XLA Modules:
  0.0 489.9 jit_solution(920126779956564696)
XLA Ops:
  18.1 1.8 slice.96
  21.5 24.0 %all_gather.13.wo_ref = bf16[768,640]{1,0:T(8,128)(2,1)} all-gather(bf16[96,640]{1,0:T(8,128)(2,1)S(1)} %slice-done), channel_id=1, replica_groups=mesh['dp'=4,'fsdp'=8] {'fsdp'}, dimensions={0}, use_global_device_ids=true | all-gather | bytes 1105920 | tf_op jit(solution)/shard_map/all_gather | solution.py:306
  45.5 17.7 %all-gather.4.cloned.1.call-done.wq_ref.wk_ref.wv_ref = bf16[768,2048]{1,0:T(8,128)(2,1)} async-done(((bf16[96,2048]{1,0:T(8,128)(2,1)}), bf16[768,2048]{1,0:T(8,128)(2,1)}) %all-gather.4.cloned.1.call-update) | async-done | bytes 3145744 | tf_op jit(solution)/shard_map/all_gather | solution.py:306
  66.2 38.4 %shard_map.305 = (bf16[10,1280,1280]{2,1,0:T(8,128)(2,1)}, bf16[1280,640]{1,0:T(8,128)(2,1)}, f32[1280,640]{1,0:T(8,128)}, f32[1280,640]{1,0:T(8,128)}, bf16[640...) custom-call(s32[1]{0:T(128)S(6)} %copy.111.length_ref, bf16[1280,640]{1,0:T(8,128)(2,1)} %token_ref.3, ...), custom_call_target="tpu_custom_call" | custom-call | tf_op jit(solution)/shard_map/pallas_call | solution.py:82
  105.1 2.4 all-gather.6.cloned.1.call-done.w1_ref
  107.5 45.9 %all-gather.8.cloned.1.call-done.w2_ref = bf16[3072,640]{1,0:T(8,128)(2,1)} async-done(((bf16[384,640]{1,0:T(8,128)(2,1)}), bf16[3072,640]{1,0:T(8,128)(2,1)}) %all-gather.8.cloned.1.call-update) | async-done | bytes 3932176 | tf_op jit(solution)/shard_map/all_gather | solution.py:306
  153.4 39.7 %shard_map.306 = (bf16[1280,640]{1,0:T(8,128)(2,1)}, bf16[1280,640]{1,0:T(8,128)(2,1)}, bf16[1280,2240]{1,0:T(8,128)(2,1)}, bf16[1280,2240]{1,0:T(8,128)(2,1)}, ...) custom-call(s32[1]{0:T(128)S(6)} %copy.111.length_ref, ...), custom_call_target="tpu_custom_call" | custom-call | tf_op jit(solution)/shard_map/pallas_call | solution.py:197
  193.2 33.8 %shard_map.307 = (bf16[1280,640]{1,0:T(8,128)(2,1)}, bf16[1280,640]{1,0:T(8,128)(2,1)}, bf16[1280,640]{1,0:T(8,128)(2,1)}, f32[8,640]{1,0:T(8,128)}) custom-call(bf16[1280,640]{1,0:T(8,128)(2,1)} %get-tuple-element.40.grad_ref, f32[1280,640]{1,0:T(8,128)} %get-tuple-element.41.wide_ref, f32[1280,640]{1,0:T(8,128)} %get-tuple-element.42.inverse_ref, ...), custom_call_target="tpu_custom_call" | custom-call | tf_op jit(solution)/shard_map/pallas_call | solution.py:274
  227.7 3.0 fusion.11
  230.8 1.5 fusion.13
  232.3 1.5 fusion.12
  234.5 2.1 fusion.5
  236.9 3.0 copy.99
  239.9 1.4 copy-done.15
  241.3 10.7 %convolution_convert_fusion.1 = bf16[640,2240]{0,1:T(8,128)(2,1)} fusion(bf16[1280,640]{1,0:T(8,128)(2,1)S(1)} %copy-done.15, bf16[1280,2240]{1,0:T(8,128)(2,1)} %get-tuple-element.54), kind=kOutput, calls=%fused_computation.5 | convolution fusion | flops 3671449600 | bytes 10240000 | tf_op jit(solution)/shard_map/dot_general | solution.py:23
  252.0 3.9 copy.106
  256.0 2.0 pad.76.clone
  258.1 1.9 copy-done.1
  259.9 2.9 fusion.8
  264.2 7.9 %convolution_convert_fusion = bf16[2240,640]{1,0:T(8,128)(2,1)S(1)} fusion(bf16[1280,2240]{1,0:T(8,128)(2,1)} %get-tuple-element.55, bf16[1280,640]{1,0:T(8,128)(2,1)} %get-tuple-element.56), kind=kOutput, calls=%fused_computation.4 | convolution fusion | flops 3671449600 | bytes 10240000 | tf_op jit(solution)/shard_map/dot_general | solution.py:23
  272.2 2.2 pad.79
  274.4 4.7 reduce-scatter.13.cloned.1.call-done
  279.2 2.0 copy.100
  281.2 43.0 %reduce-scatter.15.cloned.1.call-done = bf16[96,2240]{1,0:T(8,128)(2,1)} async-done(((bf16[768,2240]{1,0:T(8,128)(2,1)}), bf16[96,2240]{1,0:T(8,128)(2,1)}) %reduce-scatter.15.cloned.1.call-update) | async-done | bytes 430096
  324.2 2.1 copy.102
  326.3 31.1 %reduce-scatter.9.cloned.1.call-done = bf16[96,640]{1,0:T(8,128)(2,1)} async-done(((bf16[768,640]{1,0:T(8,128)(2,1)}), bf16[96,640]{1,0:T(8,128)(2,1)}) %reduce-scatter.9.cloned.1.call-update) | async-done | bytes 122896 | tf_op jit(solution)/shard_map/reduce_scatter | solution.py:344
  357.4 48.4 %reduce-scatter.11.cloned.1.call-done = bf16[384,640]{1,0:T(8,128)(2,1)} async-done(((bf16[3072,640]{1,0:T(8,128)(2,1)}), bf16[384,640]{1,0:T(8,128)(2,1)}) %reduce-scatter.11.cloned.1.call-update) | async-done | bytes 491536 | tf_op jit(solution)/shard_map/reduce_scatter | solution.py:344
  405.9 4.2 convolution_add_fusion.2
  410.1 1.7 convolution_add_fusion.1
  411.7 2.9 fusion.3
  414.6 57.6 %all-reduce.16.cloned.1.call-done = (bf16[96,2048]{0,1:T(8,128)(2,1)}, bf16[96,640]{1,0:T(8,128)(2,1)}, bf16[96,2240]{0,1:T(8,128)(2,1)}, bf16[384,640]{1,0:T(8,128)(2,1)}) async-done(((bf16[96,2048]{0,1:T(8,128)(2,1)}, bf16[96,640]{1,0:T(8,128)(2,1)}, bf16[96,2240]{0,1:T(8,128)(2,1)}, bf16[384,640]{1,0:T(8,128)(2,1)}), (bf16[96,2048]{0,1:T(8,128)(2,1)}, bf16[96,640]{1,0:T(8,128)(2,1)}, ...) | async-done | bytes 1437712 | tf_op jit(solution)/shard_map/psum | solution.py:366
  481.2 1.5 copy.98
  (95 shorter events, 27.4 us)
Async XLA Ops:
  7.2 12.8 %copy-start.7 = (bf16[384,768]{1,0:T(8,128)(2,1)S(1)}, bf16[384,768]{1,0:T(8,128)(2,1)}, u32[]{:S(2)}) copy-start(bf16[384,768]{1,0:T(8,128)(2,1)} %param.25) | copy-start | bytes 1769476
  7.2 14.3 %slice-start = ((bf16[96,768]{1,0:T(8,128)(2,1)}), bf16[96,640]{1,0:T(8,128)(2,1)S(1)}, s32[]{:S(2)}) async-start(bf16[96,768]{1,0:T(8,128)(2,1)} %param.23), calls=%async_computation.12 | async-start | bytes 245760 | tf_op jit(solution)/shard_map/slice | solution.py:320
  7.2 56.0 %all-gather.4.cloned.1.call-start = ((), (), s32[]{:S(2)}) async-start(), calls=%async_computation.4 | async-start | bytes 3538944 | tf_op jit(solution)/shard_map/all_gather | solution.py:306
  18.0 89.5 %all-gather.6.cloned.1.call-start = ((), (), s32[]{:S(2)}) async-start(), calls=%async_computation.5 | async-start | bytes 3981312 | tf_op jit(solution)/shard_map/all_gather | solution.py:306
  19.9 133.5 %all-gather.8.cloned.1.call-start = ((), (), s32[]{:S(2)}) async-start(), calls=%async_computation.6 | async-start | bytes 4423680 | tf_op jit(solution)/shard_map/all_gather | solution.py:306
  20.8 258.4 %reduce-scatter.13.cloned.1.call-start = ((), (), s32[]{:S(2)}) async-start(), calls=%async_computation.9 | async-start | bytes 3538944
  65.6 39.0 %copy-start.9 = (f32[8,640]{1,0:T(8,128)}, f32[8,640]{1,0:T(8,128)S(1)}, u32[]{:S(2)}) copy-start(f32[8,640]{1,0:T(8,128)S(1)} %convert_bitcast_fusion.vector_ref) | copy-start | bytes 61444
  193.2 34.6 %copy-start.2 = (bf16[1280,640]{1,0:T(8,128)(2,1)S(1)}, bf16[1280,640]{1,0:T(8,128)(2,1)}, u32[]{:S(2)}) copy-start(bf16[1280,640]{1,0:T(8,128)(2,1)} %token_ref.3) | copy-start | bytes 4915204
  227.7 3.0 copy-start.13
  230.8 1.5 copy-start.3
  232.3 1.5 copy-start.10
  232.3 1.6 copy-start.11
  239.8 1.4 copy-start.15
  239.9 84.3 %reduce-scatter.15.cloned.1.call-start = ((), (), s32[]{:S(2)}) async-start(), calls=%async_computation.10 | async-start | bytes 3981312
  258.0 2.0 copy-start.1
  258.0 99.4 %reduce-scatter.9.cloned.1.call-start = ((), (), s32[]{:S(2)}) async-start(), calls=%async_computation.7 | async-start | bytes 1105920 | tf_op jit(solution)/shard_map/reduce_scatter | solution.py:344
  263.9 141.9 %reduce-scatter.11.cloned.1.call-start = ((), (), s32[]{:S(2)}) async-start(), calls=%async_computation.8 | async-start | bytes 4423680 | tf_op jit(solution)/shard_map/reduce_scatter | solution.py:344
  274.4 131.5 %copy-start = (bf16[768,2048]{1,0:T(8,128)(2,1)S(1)}, bf16[768,2048]{1,0:T(8,128)(2,1)}, u32[]{:S(2)}) copy-start(bf16[768,2048]{1,0:T(8,128)(2,1)} %all-gather.4.cloned.1.call-done.wq_ref.wk_ref.wv_ref) | copy-start | bytes 9437188
  274.4 197.8 %all-reduce.16.cloned.1.call-start = ((), (), s32[]{:S(2)}) async-start(), calls=%async_computation.11 | async-start | bytes 3424256 | tf_op jit(solution)/shard_map/psum | solution.py:366
  405.8 4.2 copy-start.4
  410.0 1.7 copy-start.14
  414.6 64.3 %copy-start.12 = (pred[768]{0:T(1024)(128)(4,1)S(1)}, pred[768]{0:T(1024)(128)(4,1)}, u32[]{:S(2)}) copy-start(pred[768]{0:T(1024)(128)(4,1)} %constant.6.clone.1) | copy-start | bytes 2308
  472.2 3.7 copy-start.8
  473.9 6.1 %copy-start.6 = (bf16[384,640]{1,0:T(8,128)(2,1)S(1)}, bf16[384,640]{1,0:T(8,128)(2,1)}, u32[]{:S(2)}) copy-start(bf16[384,640]{1,0:T(8,128)(2,1)} %get-tuple-element.145) | copy-start | bytes 1474564
  475.8 5.2 %copy-start.5 = (bf16[96,2240]{0,1:T(8,128)(2,1)S(1)}, bf16[96,2240]{0,1:T(8,128)(2,1)}, u32[]{:S(2)}) copy-start(bf16[96,2240]{0,1:T(8,128)(2,1)} %get-tuple-element.144) | copy-start | bytes 1290244
Sparse Core Ops, SparseCore 0:
  18.1 45.0 all-gather.3
  65.4 42.0 all-gather.5
  109.8 43.6 all-gather.7
  240.0 39.1 reduce-scatter.12
  281.4 42.8 reduce-scatter.14
  327.0 30.3 reduce-scatter.8
  359.7 46.0 reduce-scatter.10
  409.9 62.2 all-reduce.15
